TPU v7x, 512 devices: a whole 4x8x8 slice. The times are simulated.
512 devices in a mesh: row: 64 (over x, y, core), col: 8 (over z).
Axes of the slice: x: 4, y: 8, z: 8, core: 2. Of those that a mesh axis runs over, the one named last changes fastest.
Arguments:
- right_sides: float32 [16, 2048, 1024], P(None, 'row', 'col'), may hold values from -6 to 6
- first_panel: float32 [15, 2048, 2048], P(None, 'row', 'col'), may hold values from -0.125 to 0.125
- second_panel: float32 [14, 2048, 2048], P(None, 'row', 'col'), may hold values from -0.125 to 0.125
- inverse_transposed: float32 [2, 2048, 2048], P(None, 'row', 'col'), as said below
Outputs:
- solution: float32 [2, 2048, 1024], P(None, 'col')
- remaining: float32 [14, 2048, 1024], P(None, 'row', 'col')
Inputs may be any that keep to these rules, and one draw needn't show every extreme that they name: inverse_transposed[k, s, x] is zero where s > x (each block is the transpose of a lower triangular inverse).
All inputs are finite; a program needn't handle non-finite values.
Results may differ from a plain program's by a relative error of at most 0.000094.
Values sent between devices are 32-bit elements; how exact they have to be, the bound alone decides.
A program may use at most 64 MiB of HBM per device.

v0:
```python
import jax
import jax.numpy as jnp
from jax import lax
from jax.sharding import PartitionSpec as P


def solve_block(rows, inverse_t):
    whole = lax.all_gather(rows, "col", axis=1, tiled=True)
    term = lax.dot_general(
        inverse_t,
        whole,
        (((0,), (0,)), ((), ())),
        precision=lax.Precision.HIGHEST,
        preferred_element_type=jnp.float32,
    )
    return lax.psum(term, "row")


def apply_panel(panel, solved):
    return jnp.einsum("bij,jk->bik", panel, solved, precision=lax.Precision.HIGHEST)


def reduce_rows(partial_value):
    return lax.psum_scatter(partial_value, "col", scatter_dimension=2, tiled=True)


def shards(right_sides, first_panel, second_panel, inverse_transposed):
    first = solve_block(right_sides[0], inverse_transposed[0])
    updated = right_sides[1:] - reduce_rows(apply_panel(first_panel, first))
    second = solve_block(updated[0], inverse_transposed[1])
    remaining = updated[1:] - reduce_rows(apply_panel(second_panel, second))
    solution = jnp.stack([first, second])
    return (solution, remaining)


def solution(mesh):
    return jax.shard_map(
        shards,
        mesh=mesh,
        in_specs=(
            P(None, "row", "col"),
            P(None, "row", "col"),
            P(None, "row", "col"),
            P(None, "row", "col"),
        ),
        out_specs=(P(None, "col", None), P(None, "row", "col")),
        check_vma=False,
    )
```

profile of v0, /device:TPU:1, one launch (start us, length us, event | category | flops | bytes accessed | tf_op | source)
XLA Modules:
  0.0 557.8 jit_solution(1565389148356984162)
XLA Ops:
  7.2 0.0 copy-start
  7.2 0.0 all-reduce.3.cloned.1.call-start
  7.2 0.8 slice.19
  8.0 25.7 %all-gather = f32[1,32,1024]{2,1,0:T(8,128)S(1)} all-gather(f32[1,32,128]{2,1,0:T(8,128)S(1)} %slice.19), channel_id=2, replica_groups=mesh['row'=64,'col'=8] {'col'}, dimensions={2}, use_global_device_ids=true | all-gather | bytes 147456 | tf_op jit(solution)/shard_map/all_gather | solution.py:8
  33.7 2.8 fusion.3
  36.4 0.0 all-reduce.3.cloned.1.call-update
  36.5 0.0 reduce-scatter.3.cloned.1.call-start
  36.5 199.3 %all-reduce.3.cloned.1.call-done = f32[256,1024]{1,0:T(8,128)} async-done(((f32[256,1024]{1,0:T(8,128)}), f32[256,1024]{1,0:T(8,128)}) %all-reduce.3.cloned.1.call-update) | async-done | bytes 1048592 | tf_op jit(solution)/shard_map/psum | solution.py:16
  235.8 0.0 copy-done
  235.8 4.3 convolution_bitcast_fusion
  240.1 0.0 copy-start.3
  240.1 0.0 copy-start.4
  240.1 0.0 copy-start.5
  240.1 0.0 reduce-scatter.3.cloned.1.call-update
  240.1 0.0 all-reduce.5.cloned.1.call-start
  240.2 40.3 %reduce-scatter.3.cloned.1.call-done = f32[15,32,128]{2,1,0:T(8,128)} async-done(((f32[15,32,1024]{2,1,0:T(8,128)}), f32[15,32,128]{2,1,0:T(8,128)}) %reduce-scatter.3.cloned.1.call-update) | async-done | bytes 245776 | tf_op jit(solution)/shard_map/reduce_scatter | solution.py:24
  280.5 0.0 copy-done.3
  280.5 1.0 slice_subtract_fusion
  281.5 18.2 %all-gather.1 = f32[1,32,1024]{2,1,0:T(8,128)S(1)} all-gather(f32[1,32,128]{2,1,0:T(8,128)S(1)} %slice.24), channel_id=3, replica_groups=mesh['row'=64,'col'=8] {'col'}, dimensions={2}, use_global_device_ids=true | all-gather | bytes 147456 | tf_op jit(solution)/shard_map/all_gather | solution.py:8
  299.7 0.0 copy-done.4
  299.7 2.0 convolution_bitcast_fusion.2
  301.7 0.0 all-reduce.5.cloned.1.call-update
  301.8 0.0 copy-start.1
  301.8 0.0 reduce-scatter.5.cloned.1.call-start
  301.8 203.4 %all-reduce.5.cloned.1.call-done = f32[256,1024]{1,0:T(8,128)} async-done(((f32[256,1024]{1,0:T(8,128)}), f32[256,1024]{1,0:T(8,128)}) %all-reduce.5.cloned.1.call-update) | async-done | bytes 1048592 | tf_op jit(solution)/shard_map/psum | solution.py:16
  505.2 0.0 copy-done.5
  505.3 0.0 copy-start.2
  505.3 4.2 convolution_bitcast_fusion.1
  509.5 0.0 reduce-scatter.5.cloned.1.call-update
  509.5 0.0 copy-done.1
  509.5 0.0 copy-done.2
  509.5 1.6 pad_maximum_fusion
  511.1 38.5 %reduce-scatter.5.cloned.1.call-done = f32[14,32,128]{2,1,0:T(8,128)} async-done(((f32[14,32,1024]{2,1,0:T(8,128)}), f32[14,32,128]{2,1,0:T(8,128)}) %reduce-scatter.5.cloned.1.call-update) | async-done | bytes 229392 | tf_op jit(solution)/shard_map/reduce_scatter | solution.py:24
  549.6 1.7 slice_subtract_fusion.1
  (1 shorter events, 0.0 us)
Async XLA Ops:
  7.2 228.7 %copy-start = (f32[15,32,256]{2,1,0:T(8,128)S(1)}, f32[15,32,256]{2,1,0:T(8,128)}, u32[]{:S(2)}) copy-start(f32[15,32,256]{2,1,0:T(8,128)} %param.5) | copy-start | bytes 1474564
  7.2 228.7 %all-reduce.3.cloned.1.call-start = ((), (), s32[]{:S(2)}) async-start(), calls=%async_computation.2 | async-start | bytes 2097152 | tf_op jit(solution)/shard_map/psum | solution.py:16
  36.5 244.1 %reduce-scatter.3.cloned.1.call-start = ((), (), s32[]{:S(2)}) async-start(), calls=%async_computation.3 | async-start | bytes 2211840 | tf_op jit(solution)/shard_map/reduce_scatter | solution.py:24
  240.1 40.4 %copy-start.3 = (f32[16,32,128]{2,1,0:T(8,128)S(1)}, f32[16,32,128]{2,1,0:T(8,128)}, u32[]{:S(2)}) copy-start(f32[16,32,128]{2,1,0:T(8,128)} %param.4) | copy-start | bytes 786436
  240.1 59.6 %copy-start.4 = (f32[2,32,256]{2,1,0:T(8,128)S(1)}, f32[2,32,256]{2,1,0:T(8,128)}, u32[]{:S(2)}) copy-start(f32[2,32,256]{2,1,0:T(8,128)} %param.7) | copy-start | bytes 196612
  240.1 265.1 %copy-start.5 = (f32[14,32,256]{2,1,0:T(8,128)S(1)}, f32[14,32,256]{2,1,0:T(8,128)}, u32[]{:S(2)}) copy-start(f32[14,32,256]{2,1,0:T(8,128)} %param.6) | copy-start | bytes 1376260
  240.1 265.1 %all-reduce.5.cloned.1.call-start = ((), (), s32[]{:S(2)}) async-start(), calls=%async_computation.4 | async-start | bytes 2097152 | tf_op jit(solution)/shard_map/psum | solution.py:16
  301.8 207.7 %copy-start.1 = (f32[256,1024]{1,0:T(8,128)S(1)}, f32[256,1024]{1,0:T(8,128)}, u32[]{:S(2)}) copy-start(f32[256,1024]{1,0:T(8,128)} %all-reduce.3.cloned.1.call-done) | copy-start | bytes 3145732
  301.8 247.8 %reduce-scatter.5.cloned.1.call-start = ((), (), s32[]{:S(2)}) async-start(), calls=%async_computation.5 | async-start | bytes 2064384 | tf_op jit(solution)/shard_map/reduce_scatter | solution.py:24
  505.3 4.3 copy-start.2
Sparse Core Ops, SparseCore 0:
  36.6 199.2 all-reduce.2
  240.3 40.2 reduce-scatter.2
  301.9 203.3 all-reduce.4
  509.6 39.9 reduce-scatter.4
where the time goes:
time: 561 us; the launch traced here: 558 us
  waiting for transfers between devices  482 us (86%)
  blocking collectives  43.9 us (8%)
  between operations  13.8 us (2%)
  matrix products  13.3 us (2%)
    psum x2, waiting for transfers between devices, solve_block(): return lax.psum(term, 'row')  403 us
    reduce_scatter x2, waiting for transfers between devices, reduce_rows(): lax.psum_scatter(partial_value, 'col', scatter_dimension=2, tiled=True)  78.8 us
    all_gather x2, blocking collectives, solve_block(): whole = lax.all_gather(rows, 'col', axis=1, tiled=True)  43.9 us
  transfers between devices with their start and end apart: 4, of which 4 were waited for; matrix products, arithmetic and copies ran while one was open for 0% of the time, Pallas kernels for 0%

commit v1 on v0

v1 whole, which is shorter than its diff:
```python
import functools

import jax
import jax.numpy as jnp
from jax import lax
from jax.experimental import pallas as pl
from jax.experimental.pallas import tpu as pltpu
from jax.sharding import PartitionSpec as P

MESH = pl.DeviceIdType.MESH
F32 = jnp.float32
BF16 = jnp.bfloat16

NEAR = (1, 7, 2, 6, 3, 5, 4)
FAR = NEAR[::-1]
GROUP = ((2, 0), (2, 1), (1, 0), (3, 0), (1, 1), (3, 1), (0, 1))


def split(a):
    hi = a.astype(BF16)
    return hi, (a - hi.astype(F32)).astype(BF16)


def dot(a, b):
    return jnp.dot(a, b, preferred_element_type=F32)


def dot3(a, b):
    (ah, al), (bh, bl) = a, b
    return dot(ah, bh) + (dot(al, bh) + dot(ah, bl))


def kernel(
    rhs, pan1, pan2, inv, sol, rem,
    rz, r, m0, m1, m2, r1t, pa, pa_in, pb, pb_in, u, pc, pc_in,
    full, acc, p1h, p1l, p2h, p2l, ring1, ring2,
    s_rz, q_rz, s_m, q_m, s_r1, q_r1, s_r, q_r, s_a, q_a, s_f, q_f, s_fx, q_fx, s_fc, q_fc,
    s_b, q_b, s_u, q_u, s_c, q_c, s_s, q_s, s_sx, q_sx, s_sc, q_sc, s_1, q_1, s_2, q_2,
):
    row = lax.axis_index("row")
    c = lax.axis_index("col")
    x, y, q = row // 16, (row // 2) % 8, row % 2
    g = 2 * x + q

    def dev(gg, yy, cc):
        return (((gg // 2) * 8 + yy) * 2 + gg % 2, cc)

    def zp(d):
        return dev(g, y, (c + d) % 8)

    def yp(d):
        return dev(g, (y + d) % 8, c)

    def go(e):
        return 2 * ((x + e[0]) % 4) + (q + e[1]) % 2

    def gp(e):
        return dev(go(e), y, c)

    sent = []

    def send(src, dst, ssem, rsem, to):
        cp = pltpu.make_async_remote_copy(
            src_ref=src, dst_ref=dst, send_sem=ssem, recv_sem=rsem, device_id=to, device_id_type=MESH
        )
        cp.start()
        sent.append(cp)

    def arrived(dst, rsem):
        pltpu.make_async_remote_copy(
            src_ref=dst, dst_ref=dst, send_sem=rsem, recv_sem=rsem, device_id=zp(1), device_id_type=MESH
        ).wait_recv()

    turned = dev(c, y, g)
    moves = g != c
    barrier = pltpu.get_barrier_semaphore()
    for d in NEAR:
        pl.semaphore_signal(barrier, inc=1, device_id=zp(d), device_id_type=MESH)
        pl.semaphore_signal(barrier, inc=1, device_id=yp(d), device_id_type=MESH)
    for e in GROUP:
        pl.semaphore_signal(barrier, inc=1, device_id=gp(e), device_id_type=MESH)

    @pl.when(moves)
    def _():
        pl.semaphore_signal(barrier, inc=1, device_id=turned, device_id_type=MESH)

    pl.semaphore_wait(barrier, 21 + jnp.where(moves, 1, 0))

    for d in FAR:
        send(rhs.at[0], rz.at[c], s_rz.at[d], q_rz.at[c], zp(d))
    for i, e in enumerate(GROUP):
        send(inv.at[0], m0.at[g], s_m.at[0, i], q_m.at[0, g], gp(e))
    turn = pltpu.make_async_remote_copy(
        src_ref=rhs.at[1], dst_ref=r1t, send_sem=s_r1.at[0], recv_sem=q_r1.at[0], device_id=turned, device_id_type=MESH
    )

    @pl.when(moves)
    def _():
        turn.start()

    @pl.when(jnp.logical_not(moves))
    def _():
        r1t[...] = rhs[1]

    m0[g] = inv[0]
    m1[g] = pan1[0]
    m2[g] = inv[1]
    rz[c] = rhs[0]

    for i, e in enumerate(GROUP):
        to = go(e)

        @pl.when(to != c)
        def _():
            arrived(rz.at[to], q_rz.at[to])

        send(rz.at[to], r.at[g], s_r.at[i], q_r.at[g], gp(e))

    @pl.when(g != c)
    def _():
        arrived(rz.at[g], q_rz.at[g])

    r[g] = rz[g]
    for i, e in enumerate(GROUP):
        send(pan1.at[0], m1.at[g], s_m.at[1, i], q_m.at[1, g], gp(e))
    for i, e in enumerate(GROUP):
        send(inv.at[1], m2.at[g], s_m.at[2, i], q_m.at[2, g], gp(e))

    def split_panel(pan, first, hi, lo):
        h, l = split(pan[first:first + 14].reshape(448, 256))
        hi[...] = h
        lo[...] = l

    split_panel(pan2, 0, p2h, p2l)

    for e in GROUP:
        arrived(m0.at[go(e)], q_m.at[0, go(e)])
    m0s = split(m0[...].reshape(256, 256).T)
    for e in GROUP:
        arrived(r.at[go(e)], q_r.at[go(e)])

    def reduce_start(out, part, inn, ss, qs, peer, me):
        out[...] = part.reshape(8, 32, 128)
        for d in FAR:
            send(out.at[(me + d) % 8], inn.at[d], ss.at[d], qs.at[d], peer(d))

    def reduce_end(out, inn, qs, me):
        total = out[me]
        for d in NEAR:
            arrived(inn.at[d], qs.at[d])
            total = total + inn[d]
        return total

    reduce_start(pa, dot3(m0s, split(r[...].reshape(256, 128))), pa_in, s_a, q_a, yp, y)
    split_panel(pan1, 1, p1h, p1l)
    full[0, g, y] = reduce_end(pa, pa_in, q_a, y)
    for d in FAR:
        send(full.at[0, g, y], full.at[0, g, y], s_f.at[d], q_f.at[y], yp(d))
    for e in GROUP:
        arrived(m1.at[go(e)], q_m.at[1, go(e)])
    m1s = split(m1[...].reshape(256, 256))
    for d in NEAR:
        arrived(full.at[0, g, (y + d) % 8], q_f.at[(y + d) % 8])

    reduce_start(pb, dot3(m1s, split(full[0, g].reshape(256, 128))), pb_in, s_b, q_b, zp, c)
    for i in (2, 1, 3):
        send(full.at[0, g], full.at[0, g], s_fx.at[i], q_fx.at[i], gp((i, 0)))
    send(full.at[0, g], full.at[0, g], s_fc.at[0], q_fc.at[0], gp((0, 1)))
    for e in GROUP:
        arrived(m2.at[go(e)], q_m.at[2, go(e)])
    m2s = split(m2[...].reshape(256, 256).T)

    @pl.when(moves)
    def _():
        turn.wait()

    u[c] = r1t[...] - reduce_end(pb, pb_in, q_b, c)
    for d in FAR:
        send(u.at[c], u.at[c], s_u.at[d], q_u.at[c], zp(d))
    for i in (1, 3, 2):
        came = go((4 - i, 0))
        arrived(full.at[0, came], q_fx.at[i])
        send(full.at[0, came], full.at[0, came], s_fc.at[i], q_fc.at[i], gp((0, 1)))
    for d in NEAR:
        arrived(u.at[(c + d) % 8], q_u.at[(c + d) % 8])

    reduce_start(pc, dot3(m2s, split(u[...].reshape(256, 128))), pc_in, s_c, q_c, yp, y)
    for i in range(4):
        arrived(full.at[0, go(((4 - i) % 4, 1))], q_fc.at[i])

    def first_products(j, carry):
        b = jnp.concatenate([full[0, 2 * j].reshape(256, 128), full[0, 2 * j + 1].reshape(256, 128)], axis=1)
        o = dot3((p1h[...], p1l[...]), split(b))
        acc[2 * j] = o[:, :128].reshape(14, 32, 128)
        acc[2 * j + 1] = o[:, 128:].reshape(14, 32, 128)
        return carry

    lax.fori_loop(0, 4, first_products, 0)
    full[1, g, y] = reduce_end(pc, pc_in, q_c, y)

    def pass_on(k, yy):
        for i in (2, 1, 3):
            send(full.at[1, g, yy], full.at[1, g, yy], s_sx.at[i, k], q_sx.at[i, k], gp((i, 0)))
        send(full.at[1, g, yy], full.at[1, g, yy], s_sc.at[0, k], q_sc.at[0, k], gp((0, 1)))

    for d in FAR:
        send(full.at[1, g, y], full.at[1, g, y], s_s.at[d], q_s.at[y], yp(d))
    pass_on(0, y)
    for d in NEAR:
        yy = (y + d) % 8
        arrived(full.at[1, g, yy], q_s.at[yy])
        pass_on(d, yy)
    for d in (0, *NEAR):
        yy = (y + d) % 8
        for i in (1, 3, 2):
            came = go((4 - i, 0))
            arrived(full.at[1, came, yy], q_sx.at[i, d])
            send(full.at[1, came, yy], full.at[1, came, yy], s_sc.at[i, d], q_sc.at[i, d], gp((0, 1)))
    for d in (0, *NEAR):
        yy = (y + d) % 8
        for i in range(4):
            arrived(full.at[1, go(((4 - i) % 4, 1)), yy], q_sc.at[i, d])

    def second_products(k):
        b = split(full[1, k].reshape(256, 128))
        acc[k] += dot3((p2h[...], p2l[...]), b).reshape(14, 32, 128)

    ways = ((1, 0, 0), (-1, 1, 1))

    def at(s, n):
        return (c + s * n + 8) % 8

    def half(h):
        return pl.ds(7 * h, 7)

    def hop1(s, w, h, t):
        k = at(s, 4 - t)
        if t == 0:
            src = acc.at[k, half(h)]
        else:
            src = ring1.at[w, t - 1]
            arrived(src, q_1.at[w, t - 1])
            src[...] += acc[k, half(h)]
        send(src, ring1.at[w, t], s_1.at[w, t], q_1.at[w, t], zp(s + 8))

    def hop2(s, w, h, t):
        k = at(s, 3 - t)
        if t == 0:
            src = acc.at[k, half(1 - h)]
        else:
            src = ring2.at[w, t - 1]
            arrived(src, q_2.at[w, t - 1])
            src[...] += acc[k, half(1 - h)]
        send(src, ring2.at[w, t], s_2.at[w, t], q_2.at[w, t], zp(s + 8))

    second_products(at(1, 4))
    for s, w, h in ways:
        hop1(s, w, h, 0)
    for s, w, h in ways:
        second_products(at(s, 3))
        hop2(s, w, h, 0)
    for s, w, h in ways:
        hop1(s, w, h, 1)
    for s, w, h in ways:
        second_products(at(s, 2))
        hop2(s, w, h, 1)
    for s, w, h in ways:
        hop1(s, w, h, 2)
    for s, w, h in ways:
        second_products(at(s, 1))
        hop2(s, w, h, 2)
    for s, w, h in ways:
        hop1(s, w, h, 3)
    second_products(c)
    for i in range(2):
        for k in range(8):
            sol[i, :, 128 * k:128 * (k + 1)] = full[i, k].reshape(256, 128)
    rem[...] = rhs[2:] - acc[c]
    for s, w, h in ways:
        arrived(ring2.at[w, 2], q_2.at[w, 2])
        rem[half(1 - h)] -= ring2[w, 2]
    for s, w, h in ways:
        arrived(ring1.at[w, 3], q_1.at[w, 3])
        rem[half(h)] -= ring1[w, 3]
    for cp in sent:
        cp.wait_send()


def shards(right_sides, first_panel, second_panel, inverse_transposed):
    vmem = pl.BlockSpec(memory_space=pltpu.VMEM)

    def block(*shape):
        return pltpu.VMEM(shape, F32)

    def dma(*shape):
        return pltpu.SemaphoreType.DMA(shape)

    piece, matrix = (8, 32, 128), (8, 32, 256)
    return pl.pallas_call(
        kernel,
        out_shape=(
            jax.ShapeDtypeStruct((2, 256, 1024), F32),
            jax.ShapeDtypeStruct((14, 32, 128), F32),
        ),
        in_specs=[vmem] * 4,
        out_specs=(vmem, vmem),
        scratch_shapes=[
            block(*piece), block(*piece), block(*matrix), block(*matrix), block(*matrix), block(32, 128),
            block(*piece), block(*piece), block(*piece), block(*piece), block(*piece), block(*piece), block(*piece),
            block(2, 8, 8, 32, 128), block(8, 14, 32, 128),
            pltpu.VMEM((448, 256), BF16), pltpu.VMEM((448, 256), BF16),
            pltpu.VMEM((448, 256), BF16), pltpu.VMEM((448, 256), BF16),
            block(2, 4, 7, 32, 128), block(2, 3, 7, 32, 128),
            dma(8), dma(8), dma(3, 7), dma(3, 8), dma(1), dma(1), dma(7), dma(8), dma(8), dma(8),
            dma(8), dma(8), dma(4), dma(4), dma(4), dma(4),
            dma(8), dma(8), dma(8), dma(8), dma(8), dma(8), dma(8), dma(8),
            dma(4, 8), dma(4, 8), dma(4, 8), dma(4, 8), dma(2, 4), dma(2, 4), dma(2, 3), dma(2, 3),
        ],
        compiler_params=pltpu.CompilerParams(
            collective_id=0, has_side_effects=True, vmem_limit_bytes=48 * 1024 * 1024
        ),
        cost_estimate=pl.CostEstimate(flops=1500000000, bytes_accessed=5000000, transcendentals=0),
    )(right_sides, first_panel, second_panel, inverse_transposed)


def solution(mesh):
    return jax.shard_map(
        shards,
        mesh=mesh,
        in_specs=(
            P(None, "row", "col"),
            P(None, "row", "col"),
            P(None, "row", "col"),
            P(None, "row", "col"),
        ),
        out_specs=(P(None, "col", None), P(None, "row", "col")),
        check_vma=False,
    )
```

time: 561 us -> 93.5 us (0.17)
  waiting for transfers between devices: 482 us -> 0 us
  Pallas kernels: 0 us -> 86.7 us
  blocking collectives: 43.9 us -> 0 us
  matrix products: 13.3 us -> 0 us
  between operations: 13.8 us -> 0.65 us
    psum x2 -> x0, waiting for transfers between devices: 403 us -> none  [solve_block(): return lax.psum(term, 'row')]
    pallas_call x0 -> x1, Pallas kernels: none -> 86.7 us  [shards(): pl.pallas_call(kernel, out_shape=(jax.ShapeDtypeStruct((2, 256, 1024), F3...]
    reduce_scatter x2 -> x0, waiting for transfers between devices: 78.8 us -> none  [reduce_rows(): lax.psum_scatter(partial_value, 'col', scatter_dimension=2, tiled=True)]
    all_gather x2 -> x0, blocking collectives: 43.9 us -> none  [solve_block(): whole = lax.all_gather(rows, 'col', axis=1, tiled=True)]
    dot_general x4 -> x0, matrix products: 13.3 us -> none  [the longest x2 8.5 us: apply_panel(): jnp.einsum('bij,jk->bik', panel, solved, precision=lax.Precision.HIGHEST)]
    unnamed x12 -> x10, local copies, waits for them, and re-layouts: 0.03 us -> 5.84 us
  transfers between devices with their start and end apart: 4 -> 0, of which waited for: 4 -> 0; matrix products, arithmetic and copies ran while one was open for 0% -> 0% of each run, Pallas kernels for 0% -> 0%
where the time goes in v1:
time: 93.5 us; the launch traced here: 93.2 us
  Pallas kernels  86.7 us (93%)
  local copies, waits for them, and re-layouts  5.84 us (6%)
    pallas_call x1, Pallas kernels, shards(): pl.pallas_call(kernel, out_shape=(jax.ShapeDtypeStruct((2, 256, 1024), F3...  86.7 us
    unnamed x10, local copies, waits for them, and re-layouts  5.84 us

profile of v1, /device:TPU:1, one launch (start us, length us, event | category | flops | bytes accessed | tf_op | source)
XLA Modules:
  0.0 93.2 jit_solution(13716214910125854328)
XLA Ops:
  0.6 0.0 copy-start
  0.6 1.0 %copy-done = f32[15,32,256]{2,1,0:T(8,128)S(1)} copy-done((f32[15,32,256]{2,1,0:T(8,128)S(1)}, f32[15,32,256]{2,1,0:T(8,128)}, u32[]{:S(2)}) %copy-start) | copy-done | bytes 491544
  1.7 0.0 copy-start.1
  1.7 1.0 %copy-done.1 = f32[14,32,256]{2,1,0:T(8,128)S(1)} copy-done((f32[14,32,256]{2,1,0:T(8,128)S(1)}, f32[14,32,256]{2,1,0:T(8,128)}, u32[]{:S(2)}) %copy-start.1) | copy-done | bytes 458776
  2.7 0.0 copy-start.2
  2.7 0.9 %copy-done.2 = f32[16,32,128]{2,1,0:T(8,128)S(1)} copy-done((f32[16,32,128]{2,1,0:T(8,128)S(1)}, f32[16,32,128]{2,1,0:T(8,128)}, u32[]{:S(2)}) %copy-start.2) | copy-done | bytes 262168
  3.6 0.0 copy-start.3
  3.6 0.8 copy-done.3
  4.5 86.7 %shard_map.59 = (f32[2,256,1024]{2,1,0:T(8,128)S(1)}, f32[14,32,128]{2,1,0:T(8,128)S(1)}) custom-call(f32[16,32,128]{2,1,0:T(8,128)S(1)} %copy-done.2, f32[15,32,256]{2,1,0:T(8,128)S(1)} %copy-done, f32[14,32,256]{2,1,0:T(8,128)S(1)} %copy-done.1, f32[2,32,256]{2,1,0:T(8,128)S(1)} %copy-done.3), custom_call_target="tpu_custom_call" | custom-call | flops 1500000000 | bytes 5000000 | tf_op jit(solution)/shard_map/pallas_call | solution.py:299
  91.2 1.3 %copy.8 = f32[2,256,1024]{2,1,0:T(8,128)} copy(f32[2,256,1024]{2,1,0:T(8,128)S(1)} %get-tuple-element.4) | data formatting | bytes 4194304
  92.5 0.7 copy.9
Async XLA Ops:
  0.6 1.0 %copy-start = (f32[15,32,256]{2,1,0:T(8,128)S(1)}, f32[15,32,256]{2,1,0:T(8,128)}, u32[]{:S(2)}) copy-start(f32[15,32,256]{2,1,0:T(8,128)} %pan1.1) | copy-start | bytes 1474564
  1.7 1.0 %copy-start.1 = (f32[14,32,256]{2,1,0:T(8,128)S(1)}, f32[14,32,256]{2,1,0:T(8,128)}, u32[]{:S(2)}) copy-start(f32[14,32,256]{2,1,0:T(8,128)} %pan2.1) | copy-start | bytes 1376260
  2.7 0.9 %copy-start.2 = (f32[16,32,128]{2,1,0:T(8,128)S(1)}, f32[16,32,128]{2,1,0:T(8,128)}, u32[]{:S(2)}) copy-start(f32[16,32,128]{2,1,0:T(8,128)} %rhs.1) | copy-start | bytes 786436
  3.6 0.8 copy-start.3

commit v2 on v1

v2 whole, which is shorter than its diff:
```python
import functools

import jax
import jax.numpy as jnp
from jax import lax
from jax.experimental import pallas as pl
from jax.experimental.pallas import tpu as pltpu
from jax.sharding import PartitionSpec as P

MESH = pl.DeviceIdType.MESH
F32 = jnp.float32
BF16 = jnp.bfloat16

NEAR = (1, 7, 2, 6, 3, 5, 4)
FAR = NEAR[::-1]
SLOT = (0, 1, 3, 5, 7, 6, 4, 2)
PARTS = ((0, 1), (1, 3), (3, 5), (5, 8))
GROUP = ((2, 0), (2, 1), (1, 0), (3, 0), (1, 1), (3, 1), (0, 1))


def split(a):
    hi = a.astype(BF16)
    return hi, (a - hi.astype(F32)).astype(BF16)


def dot(a, b):
    return jnp.dot(a, b, preferred_element_type=F32)


def dot3(a, b):
    (ah, al), (bh, bl) = a, b
    return dot(ah, bh) + (dot(al, bh) + dot(ah, bl))


def kernel(
    rhs_h, pan1_h, pan2_h, inv_h, sol, rem,
    rhs, pan1, pan2, s_in, r, m0, m1, m2, r1t, pa, pa_in, pb, pb_in, u, pc, pc_in,
    full, acc, p1h, p1l, p2h, p2l, ring1, ring2,
    s_m, q_m, s_r1, q_r1, s_r, q_r, s_a, q_a, s_f, q_f, s_fx, q_fx, s_fc, q_fc,
    s_b, q_b, s_u, q_u, s_c, q_c, s_s, q_s, s_sx, q_sx, s_sc, q_sc, s_1, q_1, s_2, q_2,
):
    row = lax.axis_index("row")
    c = lax.axis_index("col")
    x, y, q = row // 16, (row // 2) % 8, row % 2
    g = 2 * x + q

    def dev(gg, yy, cc):
        return (((gg // 2) * 8 + yy) * 2 + gg % 2, cc)

    def zp(d):
        return dev(g, y, (c + d) % 8)

    def yp(d):
        return dev(g, (y + d) % 8, c)

    def go(e):
        return 2 * ((x + e[0]) % 4) + (q + e[1]) % 2

    def gp(e):
        return dev(go(e), y, c)

    sent = []

    def send(src, dst, ssem, rsem, to, when=None):
        cp = pltpu.make_async_remote_copy(
            src_ref=src, dst_ref=dst, send_sem=ssem, recv_sem=rsem, device_id=to, device_id_type=MESH
        )
        if when is None:
            cp.start()
        else:
            pl.when(when)(cp.start)
        sent.append((when, cp))

    def arrived(dst, rsem):
        pltpu.make_async_remote_copy(
            src_ref=dst, dst_ref=dst, send_sem=rsem, recv_sem=rsem, device_id=zp(1), device_id_type=MESH
        ).wait_recv()

    loads = [
        pltpu.make_async_copy(src, dst, s_in.at[i])
        for i, (src, dst) in enumerate((
            (rhs_h, rhs), (inv_h.at[0], m0.at[g]), (pan1_h.at[0], m1.at[g]), (inv_h.at[1], m2.at[g]),
            (pan2_h, pan2), (pan1_h.at[pl.ds(1, 14)], pan1),
        ))
    ]
    for load in loads:
        load.start()

    turned = dev(c, y, g)
    moves = g != c
    barrier = pltpu.get_barrier_semaphore()
    for d in NEAR:
        pl.semaphore_signal(barrier, inc=1, device_id=zp(d), device_id_type=MESH)
        pl.semaphore_signal(barrier, inc=1, device_id=yp(d), device_id_type=MESH)
    for e in GROUP:
        pl.semaphore_signal(barrier, inc=1, device_id=gp(e), device_id_type=MESH)
    for e in GROUP:
        pl.semaphore_signal(barrier, inc=1, device_id=dev(go(e), y, g), device_id_type=MESH)

    @pl.when(moves)
    def _():
        pl.semaphore_signal(barrier, inc=1, device_id=dev(g, y, g), device_id_type=MESH)

    for load in loads[:4]:
        load.wait()
    pl.semaphore_wait(barrier, 28 + jnp.where(moves, 1, 0))

    for d in FAR:
        send(rhs.at[0], r.at[g], s_r.at[d], q_r.at[g], dev(c, y, (c + d) % 8))
    here = pltpu.make_async_remote_copy(
        src_ref=rhs.at[0], dst_ref=r.at[g], send_sem=s_r.at[0], recv_sem=q_r.at[g],
        device_id=dev(c, y, c), device_id_type=MESH,
    )
    turn = pltpu.make_async_remote_copy(
        src_ref=rhs.at[1], dst_ref=r1t, send_sem=s_r1.at[0], recv_sem=q_r1.at[0], device_id=turned, device_id_type=MESH
    )

    @pl.when(moves)
    def _():
        here.start()

    @pl.when(jnp.logical_not(moves))
    def _():
        r[g] = rhs[0]
        r1t[...] = rhs[1]

    for i, e in enumerate(GROUP):
        send(m0.at[g], m0.at[g], s_m.at[0, i], q_m.at[0, g], gp(e))

    @pl.when(moves)
    def _():
        turn.start()

    for i, e in enumerate(GROUP):
        send(m1.at[g], m1.at[g], s_m.at[1, i], q_m.at[1, g], gp(e))
    for i, e in enumerate(GROUP):
        send(m2.at[g], m2.at[g], s_m.at[2, i], q_m.at[2, g], gp(e))

    def split_panel(pan, hi, lo):
        h, l = split(pan[...].reshape(448, 256))
        hi[...] = h
        lo[...] = l

    for load in loads[4:]:
        load.wait()
    split_panel(pan2, p2h, p2l)

    for e in GROUP:
        arrived(m0.at[go(e)], q_m.at[0, go(e)])
    m0s = split(m0[...].reshape(256, 256).T)
    for e in GROUP:
        arrived(r.at[go(e)], q_r.at[go(e)])

    @pl.when(moves)
    def _():
        arrived(r.at[g], q_r.at[g])

    def whole(i, k):
        d = [(n - y + 8) % 8 for n in range(8)]
        at = [jnp.where(n == 0, 0, jnp.where(n <= 4, 2 * n - 1, 16 - 2 * n)) for n in d]
        return jnp.concatenate([full[i, k, n] for n in at], axis=0)

    def reduce_start(out, part, inn, ss, qs, peer, me):
        out[...] = part.reshape(8, 32, 128)
        for d in FAR:
            send(out.at[(me + d) % 8], inn.at[d], ss.at[d], qs.at[d], peer(d))

    def reduce_end(out, inn, qs, me):
        total = out[me]
        for d in NEAR:
            arrived(inn.at[d], qs.at[d])
            total = total + inn[d]
        return total

    reduce_start(pa, dot3(m0s, split(r[...].reshape(256, 128))), pa_in, s_a, q_a, yp, y)
    split_panel(pan1, p1h, p1l)
    full[0, g, 0] = reduce_end(pa, pa_in, q_a, y)
    for d in FAR:
        send(full.at[0, g, 0], full.at[0, g, SLOT[8 - d]], s_f.at[d], q_f.at[8 - d], yp(d))
    for e in GROUP:
        arrived(m1.at[go(e)], q_m.at[1, go(e)])
    m1s = split(m1[...].reshape(256, 256))
    for d in NEAR:
        arrived(full.at[0, g, SLOT[d]], q_f.at[d])

    reduce_start(pb, dot3(m1s, split(whole(0, g))), pb_in, s_b, q_b, zp, c)
    for i in (2, 1, 3):
        send(full.at[0, g], full.at[0, g], s_fx.at[i], q_fx.at[i], gp((i, 0)))
    send(full.at[0, g], full.at[0, g], s_fc.at[0], q_fc.at[0], gp((0, 1)))
    for e in GROUP:
        arrived(m2.at[go(e)], q_m.at[2, go(e)])
    m2s = split(m2[...].reshape(256, 256).T)

    @pl.when(moves)
    def _():
        turn.wait()

    u[c] = r1t[...] - reduce_end(pb, pb_in, q_b, c)
    for d in FAR:
        send(u.at[c], u.at[c], s_u.at[d], q_u.at[c], zp(d))
    for i in (1, 3, 2):
        came = go((4 - i, 0))
        arrived(full.at[0, came], q_fx.at[i])
        send(full.at[0, came], full.at[0, came], s_fc.at[i], q_fc.at[i], gp((0, 1)))
    for d in NEAR:
        arrived(u.at[(c + d) % 8], q_u.at[(c + d) % 8])

    reduce_start(pc, dot3(m2s, split(u[...].reshape(256, 128))), pc_in, s_c, q_c, yp, y)
    for i in range(4):
        arrived(full.at[0, go(((4 - i) % 4, 1))], q_fc.at[i])

    def first_products(j, carry):
        b = jnp.concatenate([whole(0, 2 * j), whole(0, 2 * j + 1)], axis=1)
        o = dot3((p1h[...], p1l[...]), split(b))
        acc[2 * j] = o[:, :128].reshape(14, 32, 128)
        acc[2 * j + 1] = o[:, 128:].reshape(14, 32, 128)
        return carry

    lax.fori_loop(0, 4, first_products, 0)
    full[1, g, 0] = reduce_end(pc, pc_in, q_c, y)

    def soon(k):
        return (jnp.abs((k - c + 8) % 8 - 4) <= 1)

    def parts(k, n):
        lo, hi = PARTS[n] if n < 4 else (0, 8)
        return full.at[1, k, pl.ds(lo, hi - lo)]

    def pass_on(n, when):
        part = parts(g, n)
        for i in (2, 1, 3):
            send(part, part, s_sx.at[i, n], q_sx.at[i, n], gp((i, 0)), when)
        send(part, part, s_sc.at[0, n], q_sc.at[0, n], gp((0, 1)), when)

    def forward(n, when, done=False):
        for i in (1, 3, 2):
            k = go((4 - i, 0))
            part = parts(k, n)
            cp = pltpu.make_async_remote_copy(
                src_ref=part, dst_ref=part, send_sem=s_sc.at[i, n], recv_sem=q_sc.at[i, n],
                device_id=gp((0, 1)), device_id_type=MESH,
            )

            @pl.when(when(k))
            def _():
                if done:
                    cp.wait_send()
                else:
                    arrived(part, q_sx.at[i, n])
                    cp.start()

    def late(k):
        return jnp.logical_not(soon(k))

    for d in FAR:
        send(full.at[1, g, 0], full.at[1, g, SLOT[8 - d]], s_s.at[d], q_s.at[8 - d], yp(d))
    for n, (lo, hi) in enumerate(PARTS):
        for d in range(1, 8):
            if lo <= SLOT[d] < hi:
                arrived(full.at[1, g, SLOT[d]], q_s.at[d])
        pass_on(n, soon(g))
    pass_on(4, late(g))
    for n in range(4):
        forward(n, soon)

    def second_products(k):
        other = k % 2 != q
        i = (x - k // 2 + 4) % 4

        @pl.when(jnp.logical_and(other, soon(k)))
        def _():
            for n in range(4):
                arrived(parts(k, n), q_sc.at[i, n])

        @pl.when(jnp.logical_and(other, late(k)))
        def _():
            arrived(parts(k, 4), q_sc.at[i, 4])

        acc[k] += dot3((p2h[...], p2l[...]), split(whole(1, k))).reshape(14, 32, 128)

    ways = ((1, 0, 0), (-1, 1, 1))

    def half(h):
        return pl.ds(7 * h, 7)

    def hop(ring, hops, ss, qs, s, w, h, t):
        k = (c + s * (hops - t) + 8) % 8
        out = ring.at[w, t]

        @pl.when(t == 0)
        def _():
            out[...] = acc[k, half(h)]

        @pl.when(t > 0)
        def _():
            arrived(out, qs.at[w, t])
            out[...] += acc[k, half(h)]

        pltpu.make_async_remote_copy(
            src_ref=out, dst_ref=ring.at[w, t + 1], send_sem=ss.at[w, t], recv_sem=qs.at[w, t + 1],
            device_id=zp(s + 8), device_id_type=MESH,
        ).start()

    def hop1(s, w, h, t):
        hop(ring1, 4, s_1, q_1, s, w, h, t)

    def hop2(s, w, h, t):
        hop(ring2, 3, s_2, q_2, s, w, 1 - h, t)

    def step(n, carry):
        second_products((c + jnp.where(n % 2 == 1, 4 - (n + 1) // 2, 4 + n // 2)) % 8)

        @pl.when(n == 0)
        def _():
            for s, w, h in ways:
                hop1(s, w, h, 0)

        @pl.when(jnp.logical_and(n % 2 == 1, n < 7))
        def _():
            hop2(*ways[0], (n - 1) // 2)

        @pl.when(jnp.logical_and(n % 2 == 0, n > 0))
        def _():
            hop2(*ways[1], (n - 2) // 2)

        @pl.when(n == 2)
        def _():
            forward(4, late)

        @pl.when(jnp.logical_and(n % 2 == 0, n > 0))
        def _():
            for s, w, h in ways:
                hop1(s, w, h, n // 2)

        return carry

    lax.fori_loop(0, 8, step, 0)
    for i in range(2):
        for k in range(8):
            sol[i, :, 128 * k:128 * (k + 1)] = whole(i, k)
    rem[...] = rhs[2:] - acc[c]
    for s, w, h in ways:
        arrived(ring2.at[w, 3], q_2.at[w, 3])
        rem[half(1 - h)] -= ring2[w, 3]
    for s, w, h in ways:
        arrived(ring1.at[w, 4], q_1.at[w, 4])
        rem[half(h)] -= ring1[w, 4]
    for when, cp in sent:
        if when is None:
            cp.wait_send()
        else:
            pl.when(when)(cp.wait_send)
    for n in range(5):
        forward(n, soon if n < 4 else late, True)
    for ring, hops, ss in ((ring1, 4, s_1), (ring2, 3, s_2)):
        for w in range(2):
            for t in range(hops):
                pltpu.make_async_remote_copy(
                    src_ref=ring.at[w, t], dst_ref=ring.at[w, t], send_sem=ss.at[w, t], recv_sem=ss.at[w, t],
                    device_id=zp(1), device_id_type=MESH,
                ).wait_send()

    @pl.when(moves)
    def _():
        here.wait_send()


def shards(*args):
    vmem = pl.BlockSpec(memory_space=pltpu.VMEM)
    outside = pl.BlockSpec(memory_space=pltpu.HBM)

    def block(*shape):
        return pltpu.VMEM(shape, F32)

    def dma(*shape):
        return pltpu.SemaphoreType.DMA(shape)

    piece, matrix = (8, 32, 128), (8, 32, 256)
    return pl.pallas_call(
        kernel,
        out_shape=(
            jax.ShapeDtypeStruct((2, 256, 1024), F32),
            jax.ShapeDtypeStruct((14, 32, 128), F32),
        ),
        in_specs=[outside] * 4,
        out_specs=(vmem, vmem),
        scratch_shapes=[
            block(16, 32, 128), block(14, 32, 256), block(14, 32, 256), dma(6),
            block(*piece), block(*matrix), block(*matrix), block(*matrix), block(32, 128),
            block(*piece), block(*piece), block(*piece), block(*piece), block(*piece), block(*piece), block(*piece),
            block(2, 8, 8, 32, 128), block(8, 14, 32, 128),
            pltpu.VMEM((448, 256), BF16), pltpu.VMEM((448, 256), BF16),
            pltpu.VMEM((448, 256), BF16), pltpu.VMEM((448, 256), BF16),
            block(2, 5, 7, 32, 128), block(2, 4, 7, 32, 128),
            dma(3, 7), dma(3, 8), dma(1), dma(1), dma(8), dma(8), dma(8), dma(8),
            dma(8), dma(8), dma(4), dma(4), dma(4), dma(4),
            dma(8), dma(8), dma(8), dma(8), dma(8), dma(8), dma(8), dma(8),
            dma(4, 5), dma(4, 5), dma(4, 5), dma(4, 5), dma(2, 5), dma(2, 5), dma(2, 4), dma(2, 4),
        ],
        compiler_params=pltpu.CompilerParams(
            collective_id=0, has_side_effects=True, vmem_limit_bytes=32 * 1024 * 1024
        ),
        cost_estimate=pl.CostEstimate(flops=1500000000, bytes_accessed=5000000, transcendentals=0),
    )(*(pltpu.with_memory_space_constraint(v, pltpu.HBM) for v in args))


def solution(mesh):
    return jax.shard_map(
        shards,
        mesh=mesh,
        in_specs=(
            P(None, "row", "col"),
            P(None, "row", "col"),
            P(None, "row", "col"),
            P(None, "row", "col"),
        ),
        out_specs=(P(None, "col", None), P(None, "row", "col")),
        check_vma=False,
    )
```

time: 93.5 us -> 85.7 us (0.917)
  local copies, waits for them, and re-layouts: 5.84 us -> 2.01 us
  Pallas kernels: 86.7 us -> 82.9 us
    pallas_call x1, Pallas kernels: 86.7 us -> 82.9 us  [shards(): pl.pallas_call(kernel, out_shape=(jax.ShapeDtypeStruct((2, 256, 1024), F3...]
    unnamed x10 -> x2, local copies, waits for them, and re-layouts: 5.84 us -> 2.01 us
where the time goes in v2:
time: 85.7 us; the launch traced here: 85.5 us
  Pallas kernels  82.9 us (97%)
  local copies, waits for them, and re-layouts  2.01 us (2%)
    pallas_call x1, Pallas kernels, shards(): pl.pallas_call(kernel, out_shape=(jax.ShapeDtypeStruct((2, 256, 1024), F3...  82.9 us
    unnamed x2, local copies, waits for them, and re-layouts  2.01 us

profile of v2, /device:TPU:1, one launch (start us, length us, event | category | flops | bytes accessed | tf_op | source)
XLA Modules:
  0.0 85.5 jit_solution(13832082675808367166)
XLA Ops:
  0.6 82.9 %shard_map.59 = (f32[2,256,1024]{2,1,0:T(8,128)S(1)}, f32[14,32,128]{2,1,0:T(8,128)S(1)}) custom-call(f32[16,32,128]{2,1,0:T(8,128)} %rhs_h.1, f32[15,32,256]{2,1,0:T(8,128)} %pan1_h.1, f32[14,32,256]{2,1,0:T(8,128)} %pan2_h.1, f32[2,32,256]{2,1,0:T(8,128)} %inv_h.1), custom_call_target="tpu_custom_call" | custom-call | flops 1500000000 | bytes 5000000 | tf_op jit(solution)/shard_map/pallas_call | solution.py:379
  83.5 1.3 %copy.8 = f32[2,256,1024]{2,1,0:T(8,128)} copy(f32[2,256,1024]{2,1,0:T(8,128)S(1)} %get-tuple-element.4) | data formatting | bytes 4194304
  84.8 0.7 copy.9

commit v3 on v2

--- a/solution.py
+++ b/solution.py
@@ -14,7 +14,8 @@
 NEAR = (1, 7, 2, 6, 3, 5, 4)
 FAR = NEAR[::-1]
 SLOT = (0, 1, 3, 5, 7, 6, 4, 2)
-PARTS = ((0, 1), (1, 3), (3, 5), (5, 8))
+PARTS = ((0, 3), (3, 8))
+PIECES = ((0, 4), (4, 7))
 GROUP = ((2, 0), (2, 1), (1, 0), (3, 0), (1, 1), (3, 1), (0, 1))
 
 
@@ -37,7 +38,7 @@
     rhs, pan1, pan2, s_in, r, m0, m1, m2, r1t, pa, pa_in, pb, pb_in, u, pc, pc_in,
     full, acc, p1h, p1l, p2h, p2l, ring1, ring2,
     s_m, q_m, s_r1, q_r1, s_r, q_r, s_a, q_a, s_f, q_f, s_fx, q_fx, s_fc, q_fc,
-    s_b, q_b, s_u, q_u, s_c, q_c, s_s, q_s, s_sx, q_sx, s_sc, q_sc, s_1, q_1, s_2, q_2,
+    s_b, q_b, s_u, q_u, s_c, q_c, s_s, q_s, s_t, q_t, s_sx, q_sx, s_sc, q_sc, s_1, q_1, s_2, q_2,
 ):
     row = lax.axis_index("row")
     c = lax.axis_index("col")
@@ -219,87 +220,72 @@
     lax.fori_loop(0, 4, first_products, 0)
     full[1, g, 0] = reduce_end(pc, pc_in, q_c, y)
 
-    def soon(k):
-        return (jnp.abs((k - c + 8) % 8 - 4) <= 1)
-
-    def parts(k, n):
-        lo, hi = PARTS[n] if n < 4 else (0, 8)
+    far = go((2, 0))
+
+    def part(k, n):
+        lo, hi = PARTS[n]
         return full.at[1, k, pl.ds(lo, hi - lo)]
 
-    def pass_on(n, when):
-        part = parts(g, n)
-        for i in (2, 1, 3):
-            send(part, part, s_sx.at[i, n], q_sx.at[i, n], gp((i, 0)), when)
-        send(part, part, s_sc.at[0, n], q_sc.at[0, n], gp((0, 1)), when)
-
-    def forward(n, when, done=False):
-        for i in (1, 3, 2):
+    def over_y(k, ss, qs):
+        for d in FAR:
+            send(full.at[1, k, 0], full.at[1, k, SLOT[8 - d]], ss.at[d], qs.at[8 - d], yp(d))
+
+    def gathered(k, qs, n):
+        lo, hi = PARTS[n]
+        for d in NEAR:
+            if lo <= SLOT[d] < hi:
+                arrived(full.at[1, k, SLOT[d]], qs.at[d])
+
+    def to_core(i, k, n):
+        send(part(k, n), part(k, n), s_sc.at[i, n], q_sc.at[i, n], gp((0, 1)))
+
+    send(full.at[1, g, 0], full.at[1, g, 0], s_sx.at[2, 0], q_sx.at[2, 0], gp((2, 0)))
+    over_y(g, s_s, q_s)
+    arrived(full.at[1, far, 0], q_sx.at[2, 0])
+    over_y(far, s_t, q_t)
+    for n in range(2):
+        gathered(g, q_s, n)
+        for i in (1, 3):
+            send(part(g, n), part(g, n), s_sx.at[i, n], q_sx.at[i, n], gp((i, 0)))
+        to_core(0, g, n)
+    for n in range(2):
+        for i in (1, 3):
             k = go((4 - i, 0))
-            part = parts(k, n)
-            cp = pltpu.make_async_remote_copy(
-                src_ref=part, dst_ref=part, send_sem=s_sc.at[i, n], recv_sem=q_sc.at[i, n],
-                device_id=gp((0, 1)), device_id_type=MESH,
-            )
-
-            @pl.when(when(k))
-            def _():
-                if done:
-                    cp.wait_send()
-                else:
-                    arrived(part, q_sx.at[i, n])
-                    cp.start()
-
-    def late(k):
-        return jnp.logical_not(soon(k))
-
-    for d in FAR:
-        send(full.at[1, g, 0], full.at[1, g, SLOT[8 - d]], s_s.at[d], q_s.at[8 - d], yp(d))
-    for n, (lo, hi) in enumerate(PARTS):
-        for d in range(1, 8):
-            if lo <= SLOT[d] < hi:
-                arrived(full.at[1, g, SLOT[d]], q_s.at[d])
-        pass_on(n, soon(g))
-    pass_on(4, late(g))
-    for n in range(4):
-        forward(n, soon)
+            arrived(part(k, n), q_sx.at[i, n])
+            to_core(i, k, n)
+        gathered(far, q_t, n)
+        to_core(2, far, n)
 
     def second_products(k):
-        other = k % 2 != q
-        i = (x - k // 2 + 4) % 4
-
-        @pl.when(jnp.logical_and(other, soon(k)))
+        @pl.when(k % 2 != q)
         def _():
-            for n in range(4):
-                arrived(parts(k, n), q_sc.at[i, n])
-
-        @pl.when(jnp.logical_and(other, late(k)))
-        def _():
-            arrived(parts(k, 4), q_sc.at[i, 4])
+            for n in range(2):
+                arrived(part(k, n), q_sc.at[(x - k // 2 + 4) % 4, n])
 
         acc[k] += dot3((p2h[...], p2l[...]), split(whole(1, k))).reshape(14, 32, 128)
 
     ways = ((1, 0, 0), (-1, 1, 1))
-
-    def half(h):
-        return pl.ds(7 * h, 7)
 
     def hop(ring, hops, ss, qs, s, w, h, t):
         k = (c + s * (hops - t) + 8) % 8
-        out = ring.at[w, t]
-
-        @pl.when(t == 0)
-        def _():
-            out[...] = acc[k, half(h)]
-
-        @pl.when(t > 0)
-        def _():
-            arrived(out, qs.at[w, t])
-            out[...] += acc[k, half(h)]
-
-        pltpu.make_async_remote_copy(
-            src_ref=out, dst_ref=ring.at[w, t + 1], send_sem=ss.at[w, t], recv_sem=qs.at[w, t + 1],
-            device_id=zp(s + 8), device_id_type=MESH,
-        ).start()
+        for j, (lo, hi) in enumerate(PIECES):
+            here_in = ring.at[w, t, pl.ds(lo, hi - lo)]
+            own = acc.at[k, pl.ds(7 * h + lo, hi - lo)]
+
+            @pl.when(t == 0)
+            def _():
+                here_in[...] = own[...]
+
+            @pl.when(t > 0)
+            def _():
+                arrived(here_in, qs.at[w, t, j])
+                here_in[...] += own[...]
+
+            pltpu.make_async_remote_copy(
+                src_ref=here_in, dst_ref=ring.at[w, t + 1, pl.ds(lo, hi - lo)],
+                send_sem=ss.at[w, t, j], recv_sem=qs.at[w, t + 1, j],
+                device_id=zp(s + 8), device_id_type=MESH,
+            ).start()
 
     def hop1(s, w, h, t):
         hop(ring1, 4, s_1, q_1, s, w, h, t)
@@ -322,10 +308,6 @@
         @pl.when(jnp.logical_and(n % 2 == 0, n > 0))
         def _():
             hop2(*ways[1], (n - 2) // 2)
-
-        @pl.when(n == 2)
-        def _():
-            forward(4, late)
 
         @pl.when(jnp.logical_and(n % 2 == 0, n > 0))
         def _():
@@ -339,30 +321,40 @@
         for k in range(8):
             sol[i, :, 128 * k:128 * (k + 1)] = whole(i, k)
     rem[...] = rhs[2:] - acc[c]
-    for s, w, h in ways:
-        arrived(ring2.at[w, 3], q_2.at[w, 3])
-        rem[half(1 - h)] -= ring2[w, 3]
-    for s, w, h in ways:
-        arrived(ring1.at[w, 4], q_1.at[w, 4])
-        rem[half(h)] -= ring1[w, 4]
+    for ring, last, qs, other in ((ring2, 3, q_2, 1), (ring1, 4, q_1, 0)):
+        for s, w, h in ways:
+            for j, (lo, hi) in enumerate(PIECES):
+                arrived(ring.at[w, last, pl.ds(lo, hi - lo)], qs.at[w, last, j])
+                rem[pl.ds(7 * (h ^ other) + lo, hi - lo)] -= ring[w, last, lo:hi]
     for when, cp in sent:
         if when is None:
             cp.wait_send()
         else:
             pl.when(when)(cp.wait_send)
-    for n in range(5):
-        forward(n, soon if n < 4 else late, True)
     for ring, hops, ss in ((ring1, 4, s_1), (ring2, 3, s_2)):
         for w in range(2):
             for t in range(hops):
-                pltpu.make_async_remote_copy(
-                    src_ref=ring.at[w, t], dst_ref=ring.at[w, t], send_sem=ss.at[w, t], recv_sem=ss.at[w, t],
-                    device_id=zp(1), device_id_type=MESH,
-                ).wait_send()
+                for j, (lo, hi) in enumerate(PIECES):
+                    out = ring.at[w, t, pl.ds(lo, hi - lo)]
+                    pltpu.make_async_remote_copy(
+                        src_ref=out, dst_ref=out, send_sem=ss.at[w, t, j], recv_sem=ss.at[w, t, j],
+                        device_id=zp(1), device_id_type=MESH,
+                    ).wait_send()
 
     @pl.when(moves)
     def _():
         here.wait_send()
+
+
+def store(sol, rem, sol_out, rem_out, sem):
+    copies = [
+        pltpu.make_async_copy(src, dst, sem.at[i])
+        for i, (src, dst) in enumerate(((sol.at[0], sol_out.at[0]), (sol.at[1], sol_out.at[1]), (rem, rem_out)))
+    ]
+    for copy in copies:
+        copy.start()
+    for copy in copies:
+        copy.wait()
 
 
 def shards(*args):
@@ -376,7 +368,7 @@
         return pltpu.SemaphoreType.DMA(shape)
 
     piece, matrix = (8, 32, 128), (8, 32, 256)
-    return pl.pallas_call(
+    outs = pl.pallas_call(
         kernel,
         out_shape=(
             jax.ShapeDtypeStruct((2, 256, 1024), F32),
@@ -395,13 +387,23 @@
             dma(3, 7), dma(3, 8), dma(1), dma(1), dma(8), dma(8), dma(8), dma(8),
             dma(8), dma(8), dma(4), dma(4), dma(4), dma(4),
             dma(8), dma(8), dma(8), dma(8), dma(8), dma(8), dma(8), dma(8),
-            dma(4, 5), dma(4, 5), dma(4, 5), dma(4, 5), dma(2, 5), dma(2, 5), dma(2, 4), dma(2, 4),
+            dma(8), dma(8), dma(4, 2), dma(4, 2), dma(4, 2), dma(4, 2), dma(2, 5, 2), dma(2, 5, 2), dma(2, 4, 2), dma(2, 4, 2),
         ],
         compiler_params=pltpu.CompilerParams(
             collective_id=0, has_side_effects=True, vmem_limit_bytes=32 * 1024 * 1024
         ),
         cost_estimate=pl.CostEstimate(flops=1500000000, bytes_accessed=5000000, transcendentals=0),
     )(*(pltpu.with_memory_space_constraint(v, pltpu.HBM) for v in args))
+    return pl.pallas_call(
+        store,
+        out_shape=(
+            jax.ShapeDtypeStruct((2, 256, 1024), F32),
+            jax.ShapeDtypeStruct((14, 32, 128), F32),
+        ),
+        in_specs=[vmem] * 2,
+        out_specs=(pl.BlockSpec(memory_space=pl.ANY),) * 2,
+        scratch_shapes=[dma(3)],
+    )(*(pltpu.with_memory_space_constraint(v, pltpu.VMEM) for v in outs))
 
 
 def solution(mesh):

time: 85.7 us -> 84 us (0.980)
  local copies, waits for them, and re-layouts: 2.01 us -> 0 us
    unnamed x2 -> x0, local copies, waits for them, and re-layouts: 2.01 us -> none
    pallas_call x0 -> x1, Pallas kernels: none -> 1.41 us  [shards(): pl.pallas_call(store, out_shape=(jax.ShapeDtypeStruct((2, 256, 1024), F32...]
    pallas_call x1, Pallas kernels: 82.9 us -> 81.9 us  [shards(): pl.pallas_call(kernel, out_shape=(jax.ShapeDtypeStruct((2, 256, 1024), F3...]
where the time goes in v3:
time: 84 us; the launch traced here: 83.9 us
  Pallas kernels  83.3 us (99%)
    pallas_call x1, Pallas kernels, shards(): pl.pallas_call(kernel, out_shape=(jax.ShapeDtypeStruct((2, 256, 1024), F3...  81.9 us

profile of v3, /device:TPU:1, one launch (start us, length us, event | category | flops | bytes accessed | tf_op | source)
XLA Modules:
  0.0 83.9 jit_solution(7348119330228125235)
XLA Ops:
  0.6 81.9 %shard_map.59 = (f32[2,256,1024]{2,1,0:T(8,128)S(1)}, f32[14,32,128]{2,1,0:T(8,128)S(1)}) custom-call(f32[16,32,128]{2,1,0:T(8,128)} %rhs_h.1, f32[15,32,256]{2,1,0:T(8,128)} %pan1_h.1, f32[14,32,256]{2,1,0:T(8,128)} %pan2_h.1, f32[2,32,256]{2,1,0:T(8,128)} %inv_h.1), custom_call_target="tpu_custom_call" | custom-call | flops 1500000000 | bytes 5000000 | tf_op jit(solution)/shard_map/pallas_call | solution.py:371
  82.5 1.4 %shard_map.60 = (f32[2,256,1024]{2,1,0:T(8,128)}, f32[14,32,128]{2,1,0:T(8,128)}) custom-call(f32[2,256,1024]{2,1,0:T(8,128)S(1)} %get-tuple-element.4.sol, f32[14,32,128]{2,1,0:T(8,128)S(1)} %get-tuple-element.5.rem), custom_call_target="tpu_custom_call" | custom-call | tf_op jit(solution)/shard_map/pallas_call | solution.py:397

commit v4 on v3

--- a/solution.py
+++ b/solution.py
@@ -106,8 +106,11 @@
         load.wait()
     pl.semaphore_wait(barrier, 28 + jnp.where(moves, 1, 0))
 
+    def uses(block, plane):
+        return 2 * (block // 2) + y // 4 <= plane
+
     for d in FAR:
-        send(rhs.at[0], r.at[g], s_r.at[d], q_r.at[g], dev(c, y, (c + d) % 8))
+        send(rhs.at[0], r.at[g], s_r.at[d], q_r.at[g], dev(c, y, (c + d) % 8), uses(g, (c + d) % 8))
     here = pltpu.make_async_remote_copy(
         src_ref=rhs.at[0], dst_ref=r.at[g], send_sem=s_r.at[0], recv_sem=q_r.at[g],
         device_id=dev(c, y, c), device_id_type=MESH,
@@ -116,7 +119,7 @@
         src_ref=rhs.at[1], dst_ref=r1t, send_sem=s_r1.at[0], recv_sem=q_r1.at[0], device_id=turned, device_id_type=MESH
     )
 
-    @pl.when(moves)
+    @pl.when(jnp.logical_and(moves, uses(g, c)))
     def _():
         here.start()
 
@@ -126,7 +129,7 @@
         r1t[...] = rhs[1]
 
     for i, e in enumerate(GROUP):
-        send(m0.at[g], m0.at[g], s_m.at[0, i], q_m.at[0, g], gp(e))
+        send(m0.at[g], m0.at[g], s_m.at[0, i], q_m.at[0, g], gp(e), uses(g, c))
 
     @pl.when(moves)
     def _():
@@ -135,7 +138,7 @@
     for i, e in enumerate(GROUP):
         send(m1.at[g], m1.at[g], s_m.at[1, i], q_m.at[1, g], gp(e))
     for i, e in enumerate(GROUP):
-        send(m2.at[g], m2.at[g], s_m.at[2, i], q_m.at[2, g], gp(e))
+        send(m2.at[g], m2.at[g], s_m.at[2, i], q_m.at[2, g], gp(e), uses(g, c))
 
     def split_panel(pan, hi, lo):
         h, l = split(pan[...].reshape(448, 256))
@@ -146,15 +149,24 @@
         load.wait()
     split_panel(pan2, p2h, p2l)
 
-    for e in GROUP:
-        arrived(m0.at[go(e)], q_m.at[0, go(e)])
+    def arrived_or_zero(buf, n, sem, needed):
+        @pl.when(needed)
+        def _():
+            arrived(buf.at[n], sem)
+
+        @pl.when(jnp.logical_not(needed))
+        def _():
+            buf[n] = jnp.zeros(buf.shape[1:], F32)
+
+    for e in GROUP:
+        arrived_or_zero(m0, go(e), q_m.at[0, go(e)], uses(go(e), c))
     m0s = split(m0[...].reshape(256, 256).T)
     for e in GROUP:
-        arrived(r.at[go(e)], q_r.at[go(e)])
+        arrived_or_zero(r, go(e), q_r.at[go(e)], uses(go(e), c))
 
     @pl.when(moves)
     def _():
-        arrived(r.at[g], q_r.at[g])
+        arrived_or_zero(r, g, q_r.at[g], uses(g, c))
 
     def whole(i, k):
         d = [(n - y + 8) % 8 for n in range(8)]
@@ -189,7 +201,7 @@
         send(full.at[0, g], full.at[0, g], s_fx.at[i], q_fx.at[i], gp((i, 0)))
     send(full.at[0, g], full.at[0, g], s_fc.at[0], q_fc.at[0], gp((0, 1)))
     for e in GROUP:
-        arrived(m2.at[go(e)], q_m.at[2, go(e)])
+        arrived_or_zero(m2, go(e), q_m.at[2, go(e)], uses(go(e), c))
     m2s = split(m2[...].reshape(256, 256).T)
 
     @pl.when(moves)
@@ -198,13 +210,14 @@
 
     u[c] = r1t[...] - reduce_end(pb, pb_in, q_b, c)
     for d in FAR:
-        send(u.at[c], u.at[c], s_u.at[d], q_u.at[c], zp(d))
+        send(u.at[c], u.at[c], s_u.at[d], q_u.at[c], zp(d), uses(c, (c + d) % 8))
     for i in (1, 3, 2):
         came = go((4 - i, 0))
         arrived(full.at[0, came], q_fx.at[i])
         send(full.at[0, came], full.at[0, came], s_fc.at[i], q_fc.at[i], gp((0, 1)))
     for d in NEAR:
-        arrived(u.at[(c + d) % 8], q_u.at[(c + d) % 8])
+        n = (c + d) % 8
+        arrived_or_zero(u, n, q_u.at[n], uses(n, c))
 
     reduce_start(pc, dot3(m2s, split(u[...].reshape(256, 128))), pc_in, s_c, q_c, yp, y)
     for i in range(4):
@@ -341,7 +354,7 @@
                         device_id=zp(1), device_id_type=MESH,
                     ).wait_send()
 
-    @pl.when(moves)
+    @pl.when(jnp.logical_and(moves, uses(g, c)))
     def _():
         here.wait_send()
 

time: 84 us -> 83.6 us (level)
  no operation moved by 1% of the time
where the time goes in v4:
time: 83.6 us; the launch traced here: 83.5 us
  Pallas kernels  82.9 us (99%)
    pallas_call x1, Pallas kernels, shards(): pl.pallas_call(kernel, out_shape=(jax.ShapeDtypeStruct((2, 256, 1024), F3...  81.5 us

profile of v4, /device:TPU:1, one launch (start us, length us, event | category | flops | bytes accessed | tf_op | source)
XLA Modules:
  0.0 83.5 jit_solution(14550065851920853628)
XLA Ops:
  0.6 81.5 %shard_map.59 = (f32[2,256,1024]{2,1,0:T(8,128)S(1)}, f32[14,32,128]{2,1,0:T(8,128)S(1)}) custom-call(f32[16,32,128]{2,1,0:T(8,128)} %rhs_h.1, f32[15,32,256]{2,1,0:T(8,128)} %pan1_h.1, f32[14,32,256]{2,1,0:T(8,128)} %pan2_h.1, f32[2,32,256]{2,1,0:T(8,128)} %inv_h.1), custom_call_target="tpu_custom_call" | custom-call | flops 1500000000 | bytes 5000000 | tf_op jit(solution)/shard_map/pallas_call | solution.py:384
  82.1 1.4 %shard_map.60 = (f32[2,256,1024]{2,1,0:T(8,128)}, f32[14,32,128]{2,1,0:T(8,128)}) custom-call(f32[2,256,1024]{2,1,0:T(8,128)S(1)} %get-tuple-element.4.sol, f32[14,32,128]{2,1,0:T(8,128)S(1)} %get-tuple-element.5.rem), custom_call_target="tpu_custom_call" | custom-call | tf_op jit(solution)/shard_map/pallas_call | solution.py:410

commit v5 on v4

--- a/solution.py
+++ b/solution.py
@@ -314,18 +314,26 @@
             for s, w, h in ways:
                 hop1(s, w, h, 0)
 
-        @pl.when(jnp.logical_and(n % 2 == 1, n < 7))
-        def _():
-            hop2(*ways[0], (n - 1) // 2)
-
-        @pl.when(jnp.logical_and(n % 2 == 0, n > 0))
-        def _():
-            hop2(*ways[1], (n - 2) // 2)
-
-        @pl.when(jnp.logical_and(n % 2 == 0, n > 0))
-        def _():
+        @pl.when(n == 1)
+        def _():
+            hop2(*ways[0], 0)
+
+        @pl.when(n == 2)
+        def _():
+            hop2(*ways[1], 0)
+
+        @pl.when(jnp.logical_or(n == 4, n == 6))
+        def _():
+            t = n // 2 - 1
             for s, w, h in ways:
-                hop1(s, w, h, n // 2)
+                hop1(s, w, h, t)
+            for s, w, h in ways:
+                hop2(s, w, h, t)
+
+        @pl.when(n == 7)
+        def _():
+            for s, w, h in ways:
+                hop1(s, w, h, 3)
 
         return carry
 

time: 83.6 us -> 83.7 us (level)
  no operation moved by 1% of the time
where the time goes in v5:
time: 83.7 us; the launch traced here: 83.5 us
  Pallas kernels  82.9 us (99%)
    pallas_call x1, Pallas kernels, shards(): pl.pallas_call(kernel, out_shape=(jax.ShapeDtypeStruct((2, 256, 1024), F3...  81.5 us

profile of v5, /device:TPU:1, one launch (start us, length us, event | category | flops | bytes accessed | tf_op | source)
XLA Modules:
  0.0 83.5 jit_solution(13639966432276737676)
XLA Ops:
  0.6 81.5 %shard_map.59 = (f32[2,256,1024]{2,1,0:T(8,128)S(1)}, f32[14,32,128]{2,1,0:T(8,128)S(1)}) custom-call(f32[16,32,128]{2,1,0:T(8,128)} %rhs_h.1, f32[15,32,256]{2,1,0:T(8,128)} %pan1_h.1, f32[14,32,256]{2,1,0:T(8,128)} %pan2_h.1, f32[2,32,256]{2,1,0:T(8,128)} %inv_h.1), custom_call_target="tpu_custom_call" | custom-call | flops 1500000000 | bytes 5000000 | tf_op jit(solution)/shard_map/pallas_call | solution.py:392
  82.1 1.4 %shard_map.60 = (f32[2,256,1024]{2,1,0:T(8,128)}, f32[14,32,128]{2,1,0:T(8,128)}) custom-call(f32[2,256,1024]{2,1,0:T(8,128)S(1)} %get-tuple-element.4.sol, f32[14,32,128]{2,1,0:T(8,128)S(1)} %get-tuple-element.5.rem), custom_call_target="tpu_custom_call" | custom-call | tf_op jit(solution)/shard_map/pallas_call | solution.py:418
